TPU v7x, 512 devices: a whole 4x4x16 slice. The times are simulated.
512 devices in a mesh: blk: 32 (over x, z_lo), feat: 16 (over z_hi, y, core).
Axes of the slice: x: 4, y: 4, z: 16 (z_hi: 2, z_lo: 8; z = z_hi * 8 + z_lo), core: 2. Of those that a mesh axis runs over, the one named last changes fastest.
Arguments:
- values: bfloat16 [16384, 8192], P('blk', 'feat'), may hold values from -6 to 6
- scales: float32 [16384, 64], P('blk', 'feat'), may hold values from 0.25 to 4
- pairing: int32 [2], replicated, may hold values from 1 to 31
Outputs:
- similarity: float32 [2, 16384, 512], P(None, 'blk', 'feat')
All inputs are finite; a program needn't handle non-finite values.
Results may differ from a plain program's by a relative error of at most 0.017.
Values may be sent and summed in bfloat16 or wider, within the bound.
A program may use at most 64 MiB of HBM per device.

v0:
```python
import jax
import jax.numpy as jnp
from jax import lax
from jax.sharding import PartitionSpec as P

FEATURES = 8192
ROUNDS = 2


eps = 1e-06


def shortened(array):
    return jax.tree.map(lambda a: a.astype(jnp.bfloat16) if a.dtype == jnp.float32 else a, array)


def passed_along(value, axis, steps):
    count = lax.axis_size(axis)
    pairs = [(source, (source + steps) % count) for source in range(count)]
    return lax.ppermute(value, axis, pairs)


def move_level(item, amount):
    return jax.tree.map(
        lambda part, own: part.astype(own.dtype), passed_along(shortened(item), "blk", amount), item
    )


def fetch_partner(item, offset):
    blocks = lax.axis_size("blk")
    count = (blocks - 1).bit_length()
    for level in range(count):
        moved = move_level(item, blocks - (1 << level))
        flag = jnp.bitwise_and(jnp.right_shift(offset, level), 1) == 1
        item = jax.tree.map(lambda kept, came: jnp.where(flag, came, kept), item, moved)
    return item


def local(values, scales, pairing):
    rows, width = values.shape
    groups = scales.shape[1]
    wide = values.astype(jnp.float32).reshape(rows, groups, width // groups) * scales[:, :, None]
    features = wide.reshape(rows, width).astype(jnp.bfloat16)
    part_sq = jnp.sum(jnp.square(features.astype(jnp.float32)), axis=1)
    own_sq = lax.psum(part_sq, "feat")
    own_inv = lax.rsqrt(own_sq + eps)
    share = rows // lax.axis_size("feat")
    start = lax.axis_index("feat") * share
    factor = jnp.float32(FEATURES) ** 0.5
    tiles = []
    for step in range(ROUNDS):
        offset = pairing[step]
        other_feat, other_part = fetch_partner((features, part_sq), offset)
        other_sq = lax.psum(other_part, "feat")
        other_inv = lax.rsqrt(other_sq + eps)
        partial_value = lax.dot_general(
            features, other_feat, (((1,), (1,)), ((), ())), preferred_element_type=jnp.float32
        )
        gram = lax.psum_scatter(
            partial_value.astype(jnp.bfloat16), "feat", scatter_dimension=1, tiled=True
        ).astype(jnp.float32)
        columns_inv = lax.dynamic_slice_in_dim(other_inv, start, share, 0)
        tiles.append(gram * own_inv[:, None] * columns_inv[None, :] * factor)
    return jnp.stack(tiles)


def solution(mesh):
    placed = (P("blk", "feat"), P("blk", "feat"), P())
    return jax.shard_map(
        local, mesh=mesh, in_specs=placed, out_specs=P(None, "blk", "feat"), check_vma=False
    )
```

profile of v0, /device:TPU:6, one launch (start us, length us, event | category | flops | bytes accessed | tf_op | source)
XLA Modules:
  0.0 422.5 jit_solution(13870914427260381237)
XLA Ops:
  6.5 0.0 reduce-scatter.5.cloned.1.call-start
  6.5 0.8 copy.4
  7.4 0.0 copy-start
  7.4 0.6 mul.54
  8.0 0.4 copy-done
  8.4 0.2 multiply_reduce_fusion
  8.7 0.0 copy-start.1
  8.7 13.4 %collective-permute-start = (bf16[512,512]{1,0:T(8,128)(2,1)S(1)}, bf16[512,512]{1,0:T(8,128)(2,1)S(1)}, u32[]{:S(2)}, u32[]{:S(2)}) collective-permute-start(bf16[512,512]{1,0:T(8,128)(2,1)S(1)} %get-tuple-element.13), channel_id=1, source_target_pairs={{0,496},{16,0},{32,16},{48,32},{64,48},{80,64},{96,80},{112,96},{1... | collective-permute-start | bytes 1572872 | tf_op jit(solution)/shard_map/ppermute | solution.py:20
  22.1 0.0 copy-done.1
  22.1 0.6 fusion.14
  24.1 9.2 %collective-permute-done = bf16[512,512]{1,0:T(8,128)(2,1)S(1)} collective-permute-done((bf16[512,512]{1,0:T(8,128)(2,1)S(1)}, bf16[512,512]{1,0:T(8,128)(2,1)S(1)}, u32[]{:S(2)}, u32[]{:S(2)}) %collective-permute-start) | collective-permute-done | bytes 524320 | tf_op jit(solution)/shard_map/ppermute | solution.py:20
  33.3 0.1 broadcast_select_fusion.4
  33.3 3.2 collective-permute-start.10
  37.2 1.9 collective-permute-start.1
  39.2 32.0 %collective-permute-done.10 = bf16[512,512]{1,0:T(8,128)(2,1)S(1)} collective-permute-done((bf16[512,512]{1,0:T(8,128)(2,1)S(1)}, bf16[512,512]{1,0:T(8,128)(2,1)S(1)}, u32[]{:S(2)}, u32[]{:S(2)}) %collective-permute-start.10) | collective-permute-done | bytes 524320 | tf_op jit(solution)/shard_map/ppermute | solution.py:20
  71.1 0.1 broadcast_select_fusion.1
  71.2 3.2 collective-permute-start.11
  75.7 7.4 %collective-permute-done.1 = bf16[512,512]{1,0:T(8,128)(2,1)S(1)} collective-permute-done((bf16[512,512]{1,0:T(8,128)(2,1)S(1)}, bf16[512,512]{1,0:T(8,128)(2,1)S(1)}, u32[]{:S(2)}, u32[]{:S(2)}) %collective-permute-start.1) | collective-permute-done | bytes 524320 | tf_op jit(solution)/shard_map/ppermute | solution.py:20
  83.1 0.1 broadcast_select_fusion.5
  83.2 13.8 %collective-permute-start.2 = (bf16[512,512]{1,0:T(8,128)(2,1)S(1)}, bf16[512,512]{1,0:T(8,128)(2,1)S(1)}, u32[]{:S(2)}, u32[]{:S(2)}) collective-permute-start(bf16[512,512]{1,0:T(8,128)(2,1)S(1)} %broadcast_select_fusion.5), channel_id=1, source_target_pairs={{0,448},{16,464},{32,480},{48,496},{64,0},{80,16},{96,32},{112,48}... | collective-permute-start | bytes 1572872 | tf_op jit(solution)/shard_map/ppermute | solution.py:20
  97.0 61.9 %collective-permute-done.11 = bf16[512,512]{1,0:T(8,128)(2,1)S(1)} collective-permute-done((bf16[512,512]{1,0:T(8,128)(2,1)S(1)}, bf16[512,512]{1,0:T(8,128)(2,1)S(1)}, u32[]{:S(2)}, u32[]{:S(2)}) %collective-permute-start.11) | collective-permute-done | bytes 524320 | tf_op jit(solution)/shard_map/ppermute | solution.py:20
  158.8 0.1 broadcast_select_fusion.2
  158.9 2.7 collective-permute-start.12
  161.6 12.3 %collective-permute-start.5 = (bf16[512]{0:T(512)(128)(2,1)S(1)}, bf16[512]{0:T(512)(128)(2,1)S(1)}, u32[]{:S(2)}, u32[]{:S(2)}) collective-permute-start(bf16[512]{0:T(512)(128)(2,1)S(1)} %convert_element_type.82), channel_id=1, source_target_pairs={{0,496},{16,0},{32,16},{48,32},{64,48},{80,64},{96,80},{112,96},{1... | collective-permute-start | bytes 3080 | tf_op jit(solution)/shard_map/ppermute | solution.py:20
  175.3 0.0 collective-permute-done.2
  175.3 0.1 broadcast_select_fusion.6
  175.4 2.4 collective-permute-start.3
  177.8 0.0 collective-permute-done.12
  177.8 0.1 broadcast_select_fusion.3
  177.9 5.9 %collective-permute-start.13 = (bf16[512,512]{1,0:T(8,128)(2,1)S(1)}, bf16[512,512]{1,0:T(8,128)(2,1)S(1)}, u32[]{:S(2)}, u32[]{:S(2)}) collective-permute-start(bf16[512,512]{1,0:T(8,128)(2,1)S(1)} %broadcast_select_fusion.3), channel_id=1, source_target_pairs={{0,256},{16,272},{32,288},{48,304},{64,320},{80,336},{96,352},{112... | collective-permute-start | bytes 1572872 | tf_op jit(solution)/shard_map/ppermute | solution.py:20
  183.8 0.0 collective-permute-done.5
  183.9 1.9 collective-permute-start.14
  185.8 1.9 collective-permute-start.6
  189.0 1.2 collective-permute-done.14
  190.2 1.9 collective-permute-done.6
  192.2 4.7 %collective-permute-start.15 = (bf16[512]{0:T(512)(128)(2,1)S(1)}, bf16[512]{0:T(512)(128)(2,1)S(1)}, u32[]{:S(2)}, u32[]{:S(2)}) collective-permute-start(bf16[512]{0:T(512)(128)(2,1)S(1)} %get-tuple-element.19), channel_id=1, source_target_pairs={{0,448},{16,464},{32,480},{48,496},{64,0},{80,16},{96,32},{112,48}... | collective-permute-start | bytes 3080 | tf_op jit(solution)/shard_map/ppermute | solution.py:20
  196.9 4.4 %collective-permute-start.7 = (bf16[512]{0:T(512)(128)(2,1)S(1)}, bf16[512]{0:T(512)(128)(2,1)S(1)}, u32[]{:S(2)}, u32[]{:S(2)}) collective-permute-start(bf16[512]{0:T(512)(128)(2,1)S(1)} %get-tuple-element.18), channel_id=1, source_target_pairs={{0,448},{16,464},{32,480},{48,496},{64,0},{80,16},{96,32},{112,48}... | collective-permute-start | bytes 3080 | tf_op jit(solution)/shard_map/ppermute | solution.py:20
  201.3 0.0 collective-permute-done.3
  201.3 0.1 broadcast_select_fusion.7
  201.4 6.8 %collective-permute-start.4 = (bf16[512,512]{1,0:T(8,128)(2,1)S(1)}, bf16[512,512]{1,0:T(8,128)(2,1)S(1)}, u32[]{:S(2)}, u32[]{:S(2)}) collective-permute-start(bf16[512,512]{1,0:T(8,128)(2,1)S(1)} %broadcast_select_fusion.7), channel_id=1, source_target_pairs={{0,256},{16,272},{32,288},{48,304},{64,320},{80,336},{96,352},{112... | collective-permute-start | bytes 1572872 | tf_op jit(solution)/shard_map/ppermute | solution.py:20
  208.2 0.0 collective-permute-done.13
  208.2 1.3 convolution_convert_fusion
  209.5 0.0 reduce-scatter.5.cloned.1.call-update
  209.5 0.0 reduce-scatter.3.cloned.1.call-start
  209.5 0.0 collective-permute-done.15
  209.5 0.0 collective-permute-done.7
  209.6 1.9 collective-permute-start.8
  212.2 2.6 collective-permute-start.16
  214.8 3.1 collective-permute-done.8
  217.9 2.7 collective-permute-start.9
  220.7 0.0 collective-permute-done.16
  220.7 4.6 %collective-permute-start.17 = (bf16[512]{0:T(512)(128)(2,1)S(1)}, bf16[512]{0:T(512)(128)(2,1)S(1)}, u32[]{:S(2)}, u32[]{:S(2)}) collective-permute-start(bf16[512]{0:T(512)(128)(2,1)S(1)} %fusion.8), channel_id=1, source_target_pairs={{0,256},{16,272},{32,288},{48,304},{64,320},{80,336},{96,352},{112... | collective-permute-start | bytes 3080 | tf_op jit(solution)/shard_map/ppermute | solution.py:20
  225.3 0.0 collective-permute-done.4
  225.3 1.3 convolution_convert_fusion.1
  226.6 0.0 reduce-scatter.3.cloned.1.call-update
  226.6 0.0 collective-permute-done.9
  226.7 1.0 collective-permute-done.17
  227.7 71.1 %all-reduce = (f32[512]{0:T(512)S(1)}, f32[512]{0:T(512)S(1)}, f32[512]{0:T(512)S(1)}) all-reduce(f32[512]{0:T(512)S(1)} %convert_select_fusion.2, f32[512]{0:T(512)S(1)} %get-tuple-element.12, f32[512]{0:T(512)S(1)} %convert_select_fusion.6), channel_id=1, replica_groups=mesh['blk'=32,'feat'=16] {'feat'}, use_global_device_ids=true, to_apply=%region_5.6 | all-reduce | flops 1536 | bytes 12288 | tf_op jit(solution)/shard_map/psum | solution.py:54
  298.8 0.1 dynamic_slice.7
  298.9 0.1 dynamic_slice.6
  299.0 18.6 %reduce-scatter.5.cloned.1.call-done = bf16[512,32]{0,1:T(8,128)(2,1)} async-done(((bf16[512,512]{0,1:T(8,128)(2,1)}), bf16[512,32]{0,1:T(8,128)(2,1)}) %reduce-scatter.5.cloned.1.call-update) | async-done | bytes 32784 | tf_op jit(solution)/shard_map/reduce_scatter | solution.py:59
  317.5 96.6 %reduce-scatter.3.cloned.1.call-done = bf16[512,32]{0,1:T(8,128)(2,1)} async-done(((bf16[512,512]{0,1:T(8,128)(2,1)}), bf16[512,32]{0,1:T(8,128)(2,1)}) %reduce-scatter.3.cloned.1.call-update) | async-done | bytes 32784 | tf_op jit(solution)/shard_map/reduce_scatter | solution.py:59
  414.1 0.9 multiply_bitcast_fusion.1
  415.0 0.7 pad_maximum_fusion
  (10 shorter events, 0.1 us)
Async XLA Ops:
  6.5 311.0 %reduce-scatter.5.cloned.1.call-start = ((), (), s32[]{:S(2)}) async-start(), calls=%async_computation.3 | async-start | bytes 557056 | tf_op jit(solution)/shard_map/reduce_scatter | solution.py:59
  7.4 1.0 copy-start
  8.7 13.4 %copy-start.1 = (s32[2]{0:T(128)S(1)}, s32[2]{0:T(128)}, u32[]{:S(2)}) copy-start(s32[2]{0:T(128)} %param.5) | copy-start | bytes 28
  8.7 24.6 %collective-permute-start = (bf16[512,512]{1,0:T(8,128)(2,1)S(1)}, bf16[512,512]{1,0:T(8,128)(2,1)S(1)}, u32[]{:S(2)}, u32[]{:S(2)}) collective-permute-start(bf16[512,512]{1,0:T(8,128)(2,1)S(1)} %get-tuple-element.13), channel_id=1, source_target_pairs={{0,496},{16,0},{32,16},{48,32},{64,48},{80,64},{96,80},{112,96},{1... | collective-permute-start | bytes 1572872 | tf_op jit(solution)/shard_map/ppermute | solution.py:20
  33.3 37.8 %collective-permute-start.10 = (bf16[512,512]{1,0:T(8,128)(2,1)S(1)}, bf16[512,512]{1,0:T(8,128)(2,1)S(1)}, u32[]{:S(2)}, u32[]{:S(2)}) collective-permute-start(bf16[512,512]{1,0:T(8,128)(2,1)S(1)} %get-tuple-element.15), channel_id=1, source_target_pairs={{0,480},{16,496},{32,0},{48,16},{64,32},{80,48},{96,64},{112,80},{... | collective-permute-start | bytes 1572872 | tf_op jit(solution)/shard_map/ppermute | solution.py:20
  37.2 45.9 %collective-permute-start.1 = (bf16[512,512]{1,0:T(8,128)(2,1)S(1)}, bf16[512,512]{1,0:T(8,128)(2,1)S(1)}, u32[]{:S(2)}, u32[]{:S(2)}) collective-permute-start(bf16[512,512]{1,0:T(8,128)(2,1)S(1)} %get-tuple-element.14), channel_id=1, source_target_pairs={{0,480},{16,496},{32,0},{48,16},{64,32},{80,48},{96,64},{112,80},{... | collective-permute-start | bytes 1572872 | tf_op jit(solution)/shard_map/ppermute | solution.py:20
  71.2 87.7 %collective-permute-start.11 = (bf16[512,512]{1,0:T(8,128)(2,1)S(1)}, bf16[512,512]{1,0:T(8,128)(2,1)S(1)}, u32[]{:S(2)}, u32[]{:S(2)}) collective-permute-start(bf16[512,512]{1,0:T(8,128)(2,1)S(1)} %broadcast_select_fusion.1), channel_id=1, source_target_pairs={{0,448},{16,464},{32,480},{48,496},{64,0},{80,16},{96,32},{112,48}... | collective-permute-start | bytes 1572872 | tf_op jit(solution)/shard_map/ppermute | solution.py:20
  83.2 92.1 %collective-permute-start.2 = (bf16[512,512]{1,0:T(8,128)(2,1)S(1)}, bf16[512,512]{1,0:T(8,128)(2,1)S(1)}, u32[]{:S(2)}, u32[]{:S(2)}) collective-permute-start(bf16[512,512]{1,0:T(8,128)(2,1)S(1)} %broadcast_select_fusion.5), channel_id=1, source_target_pairs={{0,448},{16,464},{32,480},{48,496},{64,0},{80,16},{96,32},{112,48}... | collective-permute-start | bytes 1572872 | tf_op jit(solution)/shard_map/ppermute | solution.py:20
  158.9 18.9 %collective-permute-start.12 = (bf16[512,512]{1,0:T(8,128)(2,1)S(1)}, bf16[512,512]{1,0:T(8,128)(2,1)S(1)}, u32[]{:S(2)}, u32[]{:S(2)}) collective-permute-start(bf16[512,512]{1,0:T(8,128)(2,1)S(1)} %broadcast_select_fusion.2), channel_id=1, source_target_pairs={{0,384},{16,400},{32,416},{48,432},{64,448},{80,464},{96,480},{112... | collective-permute-start | bytes 1572872 | tf_op jit(solution)/shard_map/ppermute | solution.py:20
  161.6 22.2 %collective-permute-start.5 = (bf16[512]{0:T(512)(128)(2,1)S(1)}, bf16[512]{0:T(512)(128)(2,1)S(1)}, u32[]{:S(2)}, u32[]{:S(2)}) collective-permute-start(bf16[512]{0:T(512)(128)(2,1)S(1)} %convert_element_type.82), channel_id=1, source_target_pairs={{0,496},{16,0},{32,16},{48,32},{64,48},{80,64},{96,80},{112,96},{1... | collective-permute-start | bytes 3080 | tf_op jit(solution)/shard_map/ppermute | solution.py:20
  175.4 25.9 %collective-permute-start.3 = (bf16[512,512]{1,0:T(8,128)(2,1)S(1)}, bf16[512,512]{1,0:T(8,128)(2,1)S(1)}, u32[]{:S(2)}, u32[]{:S(2)}) collective-permute-start(bf16[512,512]{1,0:T(8,128)(2,1)S(1)} %broadcast_select_fusion.6), channel_id=1, source_target_pairs={{0,384},{16,400},{32,416},{48,432},{64,448},{80,464},{96,480},{112... | collective-permute-start | bytes 1572872 | tf_op jit(solution)/shard_map/ppermute | solution.py:20
  177.9 30.3 %collective-permute-start.13 = (bf16[512,512]{1,0:T(8,128)(2,1)S(1)}, bf16[512,512]{1,0:T(8,128)(2,1)S(1)}, u32[]{:S(2)}, u32[]{:S(2)}) collective-permute-start(bf16[512,512]{1,0:T(8,128)(2,1)S(1)} %broadcast_select_fusion.3), channel_id=1, source_target_pairs={{0,256},{16,272},{32,288},{48,304},{64,320},{80,336},{96,352},{112... | collective-permute-start | bytes 1572872 | tf_op jit(solution)/shard_map/ppermute | solution.py:20
  183.9 6.4 %collective-permute-start.14 = (bf16[512]{0:T(512)(128)(2,1)S(1)}, bf16[512]{0:T(512)(128)(2,1)S(1)}, u32[]{:S(2)}, u32[]{:S(2)}) collective-permute-start(bf16[512]{0:T(512)(128)(2,1)S(1)} %get-tuple-element.21), channel_id=1, source_target_pairs={{0,480},{16,496},{32,0},{48,16},{64,32},{80,48},{96,64},{112,80},{... | collective-permute-start | bytes 3080 | tf_op jit(solution)/shard_map/ppermute | solution.py:20
  185.8 6.4 %collective-permute-start.6 = (bf16[512]{0:T(512)(128)(2,1)S(1)}, bf16[512]{0:T(512)(128)(2,1)S(1)}, u32[]{:S(2)}, u32[]{:S(2)}) collective-permute-start(bf16[512]{0:T(512)(128)(2,1)S(1)} %get-tuple-element.20), channel_id=1, source_target_pairs={{0,480},{16,496},{32,0},{48,16},{64,32},{80,48},{96,64},{112,80},{... | collective-permute-start | bytes 3080 | tf_op jit(solution)/shard_map/ppermute | solution.py:20
  192.2 17.4 %collective-permute-start.15 = (bf16[512]{0:T(512)(128)(2,1)S(1)}, bf16[512]{0:T(512)(128)(2,1)S(1)}, u32[]{:S(2)}, u32[]{:S(2)}) collective-permute-start(bf16[512]{0:T(512)(128)(2,1)S(1)} %get-tuple-element.19), channel_id=1, source_target_pairs={{0,448},{16,464},{32,480},{48,496},{64,0},{80,16},{96,32},{112,48}... | collective-permute-start | bytes 3080 | tf_op jit(solution)/shard_map/ppermute | solution.py:20
  196.9 12.7 %collective-permute-start.7 = (bf16[512]{0:T(512)(128)(2,1)S(1)}, bf16[512]{0:T(512)(128)(2,1)S(1)}, u32[]{:S(2)}, u32[]{:S(2)}) collective-permute-start(bf16[512]{0:T(512)(128)(2,1)S(1)} %get-tuple-element.18), channel_id=1, source_target_pairs={{0,448},{16,464},{32,480},{48,496},{64,0},{80,16},{96,32},{112,48}... | collective-permute-start | bytes 3080 | tf_op jit(solution)/shard_map/ppermute | solution.py:20
  201.4 23.9 %collective-permute-start.4 = (bf16[512,512]{1,0:T(8,128)(2,1)S(1)}, bf16[512,512]{1,0:T(8,128)(2,1)S(1)}, u32[]{:S(2)}, u32[]{:S(2)}) collective-permute-start(bf16[512,512]{1,0:T(8,128)(2,1)S(1)} %broadcast_select_fusion.7), channel_id=1, source_target_pairs={{0,256},{16,272},{32,288},{48,304},{64,320},{80,336},{96,352},{112... | collective-permute-start | bytes 1572872 | tf_op jit(solution)/shard_map/ppermute | solution.py:20
  209.5 204.7 %reduce-scatter.3.cloned.1.call-start = ((), (), s32[]{:S(2)}) async-start(), calls=%async_computation.2 | async-start | bytes 557056 | tf_op jit(solution)/shard_map/reduce_scatter | solution.py:59
  209.6 8.4 %collective-permute-start.8 = (bf16[512]{0:T(512)(128)(2,1)S(1)}, bf16[512]{0:T(512)(128)(2,1)S(1)}, u32[]{:S(2)}, u32[]{:S(2)}) collective-permute-start(bf16[512]{0:T(512)(128)(2,1)S(1)} %get-tuple-element.8), channel_id=1, source_target_pairs={{0,384},{16,400},{32,416},{48,432},{64,448},{80,464},{96,480},{112... | collective-permute-start | bytes 3080 | tf_op jit(solution)/shard_map/ppermute | solution.py:20
  212.2 8.5 %collective-permute-start.16 = (bf16[512]{0:T(512)(128)(2,1)S(1)}, bf16[512]{0:T(512)(128)(2,1)S(1)}, u32[]{:S(2)}, u32[]{:S(2)}) collective-permute-start(bf16[512]{0:T(512)(128)(2,1)S(1)} %get-tuple-element.16), channel_id=1, source_target_pairs={{0,384},{16,400},{32,416},{48,432},{64,448},{80,464},{96,480},{112... | collective-permute-start | bytes 3080 | tf_op jit(solution)/shard_map/ppermute | solution.py:20
  217.9 8.7 %collective-permute-start.9 = (bf16[512]{0:T(512)(128)(2,1)S(1)}, bf16[512]{0:T(512)(128)(2,1)S(1)}, u32[]{:S(2)}, u32[]{:S(2)}) collective-permute-start(bf16[512]{0:T(512)(128)(2,1)S(1)} %fusion.6), channel_id=1, source_target_pairs={{0,256},{16,272},{32,288},{48,304},{64,320},{80,336},{96,352},{112... | collective-permute-start | bytes 3080 | tf_op jit(solution)/shard_map/ppermute | solution.py:20
  220.7 7.0 %collective-permute-start.17 = (bf16[512]{0:T(512)(128)(2,1)S(1)}, bf16[512]{0:T(512)(128)(2,1)S(1)}, u32[]{:S(2)}, u32[]{:S(2)}) collective-permute-start(bf16[512]{0:T(512)(128)(2,1)S(1)} %fusion.8), channel_id=1, source_target_pairs={{0,256},{16,272},{32,288},{48,304},{64,320},{80,336},{96,352},{112... | collective-permute-start | bytes 3080 | tf_op jit(solution)/shard_map/ppermute | solution.py:20
Sparse Core Ops, SparseCore 0:
  209.6 107.8 reduce-scatter.4
  322.9 91.2 reduce-scatter.2
where the time goes:
time: 423 us; the launch traced here: 422 us
  waiting for transfers between devices  233 us (55%)
  starting transfers between devices  90.7 us (21%)
  blocking collectives  71.1 us (17%)
  between operations  20.4 us (5%)
    ppermute x18, waiting for transfers between devices, passed_along(): return lax.ppermute(value, axis, pairs)  118 us
    reduce_scatter x2, waiting for transfers between devices, local(): lax.psum_scatter(partial_value.astype(jnp.bfloat16), 'feat', scatter_dime...  115 us
    ppermute x18, starting transfers between devices, passed_along(): return lax.ppermute(value, axis, pairs)  90.7 us
    psum x1, blocking collectives, local(): other_sq = lax.psum(other_part, 'feat')  71.1 us
  transfers between devices with their start and end apart: 20, of which 10 were waited for; matrix products, arithmetic and copies ran while one was open for 1% of the time, Pallas kernels for 0%

commit v1 on v0

v1 whole, which is shorter than its diff:
```python
import functools

import jax
import jax.numpy as jnp
from jax import lax
from jax.experimental import pallas as pl
from jax.experimental.pallas import tpu as pltpu
from jax.sharding import PartitionSpec as P

FEATURES = 8192
ROUNDS = 2
EPS = 1e-06
N_BLK = 32
MESH = pl.DeviceIdType.MESH


def fetch_kernel(offset, pieces, src, dst, send, recv):
    blk = lax.axis_index("blk")
    source = lax.rem(blk + offset, N_BLK)
    target = lax.rem(blk + (N_BLK - offset), N_BLK)
    barrier = pltpu.get_barrier_semaphore()
    pl.semaphore_signal(barrier, inc=1, device_id={"blk": source}, device_id_type=MESH)
    pl.semaphore_wait(barrier, 1)
    rows = src.shape[0] // pieces
    copies = []
    for piece in range(pieces):
        part = pl.ds(piece * rows, rows)
        copy = pltpu.make_async_remote_copy(
            src_ref=src.at[part], dst_ref=dst.at[part], send_sem=send.at[piece], recv_sem=recv.at[piece],
            device_id={"blk": target}, device_id_type=MESH,
        )
        copy.start()
        copies.append(copy)
    for copy in copies:
        copy.wait()


def fetch(offset, features):
    pieces = 1
    return pl.pallas_call(
        functools.partial(fetch_kernel, offset, pieces),
        out_shape=jax.ShapeDtypeStruct(features.shape, features.dtype),
        in_specs=[pl.BlockSpec(memory_space=pl.ANY)],
        out_specs=pl.BlockSpec(memory_space=pl.ANY),
        scratch_shapes=[pltpu.SemaphoreType.DMA((pieces,)), pltpu.SemaphoreType.DMA((pieces,))],
        compiler_params=pltpu.CompilerParams(collective_id=offset, has_side_effects=True),
        name=f"fetch_{offset}",
    )(features)


def dot_t(a, b):
    return lax.dot_general(a, b, (((1,), (1,)), ((), ())), preferred_element_type=jnp.float32)


def square_sums(block):
    wide = block.astype(jnp.float32)
    square = wide * wide
    high = square.astype(jnp.bfloat16)
    low = (square - high.astype(jnp.float32)).astype(jnp.bfloat16)
    ones = jnp.ones((8, block.shape[1]), jnp.bfloat16)
    return dot_t(ones, high) + dot_t(ones, low)


def gram_kernel(own_ref, first_ref, second_ref, out_ref,
                mine, s1, r1, s2, r2, s3, r3, n0, n1, n2, n3,
                send1, recv1, send2, recv2, send3, recv3):
    feat = lax.axis_index("feat")
    core = lax.rem(feat, 2)
    y = lax.rem(feat // 2, 4)
    half = feat // 8
    to_core = feat + 1 - 2 * core
    to_half = feat + 8 - 16 * half
    to_y = [feat + 2 * (lax.rem(y + t, 4) - y) for t in (1, 2, 3)]

    barrier = pltpu.get_barrier_semaphore()
    for peer in [to_core, to_half] + to_y:
        pl.semaphore_signal(barrier, inc=1, device_id={"feat": peer}, device_id_type=MESH)
    partners = (first_ref, second_ref)

    def remote(src, dst, send, recv, peer):
        return pltpu.make_async_remote_copy(
            src_ref=src, dst_ref=dst, send_sem=send, recv_sem=recv,
            device_id={"feat": peer}, device_id_type=MESH)

    own = own_ref[...]
    stage1 = []
    for r in range(ROUNDS):
        rows = partners[r][:, 1 - core].reshape(256, 512)
        s1[r] = dot_t(rows, own).astype(jnp.bfloat16).reshape(8, 32, 512)
        if r == 0:
            pl.semaphore_wait(barrier, 5)
        copy = remote(s1.at[r], r1.at[r], send1.at[r], recv1.at[r], to_core)
        copy.start()
        stage1.append(copy)
    row = lax.broadcasted_iota(jnp.int32, (8, 512), 0)
    sums = [square_sums(own)] + [square_sums(p[...].reshape(512, 512)) for p in partners]
    n0[...] = jnp.where(row == 0, sums[0], jnp.where(row == 1, sums[1], sums[2]))
    copy = remote(n0, n1.at[0], send1.at[2], recv1.at[2], to_core)
    copy.start()
    stage1.append(copy)
    for r in range(ROUNDS):
        rows = partners[r][:, core].reshape(256, 512)
        mine[r] = dot_t(rows, own).reshape(8, 32, 512)

    for copy in stage1:
        copy.wait_recv()
    stage2 = []
    n1[1] = n0[...] + n1[0]
    for t in (1, 2, 3):
        there = lax.rem(y + t, 4)
        for r in range(ROUNDS):
            for h in range(2):
                q = h * 4 + there
                s2[t - 1, r, h] = (mine[r, q] + r1[r, q].astype(jnp.float32)).astype(jnp.bfloat16)
        for src, dst, k in ((s2.at[t - 1], r2.at[t - 1], 0), (n1.at[1], n2.at[t - 1], 1)):
            copy = remote(src, dst, send2.at[t - 1, k], recv2.at[t - 1, k], to_y[t - 1])
            copy.start()
            stage2.append(copy)
    for copy in stage2:
        copy.wait_recv()

    def total(r, h):
        q = h * 4 + y
        value = mine[r, q] + r1[r, q].astype(jnp.float32)
        for t in range(3):
            value = value + r2[t, r, h].astype(jnp.float32)
        return value

    n3[0] = n1[1] + n2[0] + n2[1] + n2[2]
    for r in range(ROUNDS):
        s3[r] = total(r, 1 - half).astype(jnp.bfloat16)
    stage3 = [remote(s3, r3, send3.at[0], recv3.at[0], to_half),
              remote(n3.at[0], n3.at[1], send3.at[1], recv3.at[1], to_half)]
    for copy in stage3:
        copy.start()
    for r in range(ROUNDS):
        mine[r, 0] = total(r, half)
    for copy in stage3:
        copy.wait_recv()
    inverse = lax.rsqrt(n3[0] + n3[1] + EPS)
    lane = lax.broadcasted_iota(jnp.int32, (32, 512), 1)
    at = lax.broadcasted_iota(jnp.int32, (32, 512), 0) + feat * 32
    factor = jnp.float32(FEATURES) ** 0.5
    for r in range(ROUNDS):
        spread = jnp.broadcast_to(inverse[1 + r:2 + r], (32, 512))
        column = jnp.sum(jnp.where(lane == at, spread, 0.0), axis=1, keepdims=True)
        gram = mine[r, 0] + r3[r].astype(jnp.float32)
        out_ref[r] = gram * inverse[0:1] * column * factor
    for copy in stage1 + stage2 + stage3:
        copy.wait_send()


def grams(own, first, second):
    bf16, f32 = jnp.bfloat16, jnp.float32
    vmem = pl.BlockSpec(memory_space=pltpu.VMEM)
    return pl.pallas_call(
        gram_kernel,
        out_shape=jax.ShapeDtypeStruct((ROUNDS, 32, 512), f32),
        in_specs=[vmem] * 3,
        out_specs=vmem,
        scratch_shapes=[
            pltpu.VMEM((ROUNDS, 8, 32, 512), f32),
            pltpu.VMEM((ROUNDS, 8, 32, 512), bf16),
            pltpu.VMEM((ROUNDS, 8, 32, 512), bf16),
            pltpu.VMEM((3, ROUNDS, 2, 32, 512), bf16),
            pltpu.VMEM((3, ROUNDS, 2, 32, 512), bf16),
            pltpu.VMEM((ROUNDS, 32, 512), bf16),
            pltpu.VMEM((ROUNDS, 32, 512), bf16),
            pltpu.VMEM((8, 512), f32),
            pltpu.VMEM((2, 8, 512), f32),
            pltpu.VMEM((3, 8, 512), f32),
            pltpu.VMEM((2, 8, 512), f32),
            pltpu.SemaphoreType.DMA((3,)),
            pltpu.SemaphoreType.DMA((3,)),
            pltpu.SemaphoreType.DMA((3, 2)),
            pltpu.SemaphoreType.DMA((3, 2)),
            pltpu.SemaphoreType.DMA((2,)),
            pltpu.SemaphoreType.DMA((2,)),
        ],
        compiler_params=pltpu.CompilerParams(
            collective_id=0, has_side_effects=True, vmem_limit_bytes=32 * 1024 * 1024),
        name="grams",
    )(own, first.reshape(8, 2, 32, 512), second.reshape(8, 2, 32, 512))


def local(values, scales, pairing):
    rows, width = values.shape
    groups = scales.shape[1]
    wide = values.astype(jnp.float32).reshape(rows, groups, width // groups) * scales[:, :, None]
    features = wide.reshape(rows, width).astype(jnp.bfloat16)
    fetches = [functools.partial(fetch, offset) for offset in range(1, N_BLK)]
    others = [lax.switch(pairing[r] - 1, fetches, features) for r in range(ROUNDS)]
    tiles = grams(features, *others)
    return jnp.swapaxes(tiles, 1, 2)


def solution(mesh):
    placed = (P("blk", "feat"), P("blk", "feat"), P())
    return jax.shard_map(
        local, mesh=mesh, in_specs=placed, out_specs=P(None, "blk", "feat"), check_vma=False
    )
```

time: 423 us -> 115 us (0.27)
  the two profiles are of different devices: /device:TPU:6 before, /device:TPU:129 now
where the time goes in v1:
time: 115 us
  Pallas kernels  110 us (96%)
  local copies, waits for them, and re-layouts  3.16 us (3%)
  between operations  1.35 us (1%)
    pallas_call x2, Pallas kernels, fetch(): pl.pallas_call(functools.partial(fetch_kernel, offset, pieces), out_shape...  80.6 us
    pallas_call x1, Pallas kernels, grams(): pl.pallas_call(gram_kernel, out_shape=jax.ShapeDtypeStruct((ROUNDS, 32, 5...  29.7 us

profile of v1, /device:TPU:129, one launch (start us, length us, event | category | flops | bytes accessed | tf_op | source)
XLA Modules:
  0.0 115.1 jit_solution(16897997491989970273)
XLA Ops:
  0.0 1.3 %fusion.1 = (s32[1]{0:T(128)}, s32[1]{0:T(128)}) fusion(s32[2]{0:T(128)} %param.67), kind=kLoop, calls=%fused_computation.2 | loop fusion | bytes 16 | tf_op jit(solution)/shard_map/slice | solution.py:192
  1.3 0.0 copy-start.1
  2.6 0.0 copy-done.1
  2.6 0.1 copy.4
  2.8 0.0 copy-start
  2.8 0.6 mul.11
  3.4 0.4 copy-done
  3.8 0.2 fusion.own_ref
  4.0 28.2 %conditional.3 = (bf16[8,2,32,512]{3,2,1,0:T(8,128)(2,1)S(1)}) conditional(s32[]{:T(128)} %bitcast.63, bf16[512,512]{1,0:T(8,128)(2,1)S(1)} %fusion.own_ref, bf16[512,512]{1,0:T(8,128)(2,1)S(1)} %fusion.own_ref, bf16[512,512]{1,0:T(8,128)(2,1)S(1)} %fusion.own_ref, bf16[512,512]{1,0:T(8,128)(2,1)S(1)} %fusion.own_ref, ...), branch_computations={%region_31.0_spmd, %region_32.0_spmd, %region_33.0_spmd, %region_3... | conditional | bytes 8 | solution.py:192
  4.1 28.1 %fetch_5.3 = bf16[512,512]{1,0:T(8,128)(2,1)S(1)} custom-call(bf16[512,512]{1,0:T(8,128)(2,1)S(1)} %src.35), custom_call_target="tpu_custom_call" | custom-call | tf_op jit(solution)/shard_map/cond/branch_4_fun/fetch_5/pallas_call | solution.py:40
  32.2 52.5 %conditional.2 = (bf16[8,2,32,512]{3,2,1,0:T(8,128)(2,1)S(1)}) conditional(s32[]{:T(128)} %bitcast.62, bf16[512,512]{1,0:T(8,128)(2,1)S(1)} %fusion.own_ref, bf16[512,512]{1,0:T(8,128)(2,1)S(1)} %fusion.own_ref, bf16[512,512]{1,0:T(8,128)(2,1)S(1)} %fusion.own_ref, bf16[512,512]{1,0:T(8,128)(2,1)S(1)} %fusion.own_ref, ...), branch_computations={%region_0.0_spmd, %region_1.0_spmd, %region_2.0_spmd, %region_3.0_... | conditional | bytes 8 | solution.py:192
  32.3 52.4 %fetch_18.2 = bf16[512,512]{1,0:T(8,128)(2,1)S(1)} custom-call(bf16[512,512]{1,0:T(8,128)(2,1)S(1)} %src.17), custom_call_target="tpu_custom_call" | custom-call | tf_op jit(solution)/shard_map/cond/branch_17_fun/fetch_18/pallas_call | solution.py:40
  84.8 29.7 %grams.1 = f32[2,32,512]{2,1,0:T(8,128)S(1)} custom-call(bf16[512,512]{1,0:T(8,128)(2,1)S(1)} %fusion.own_ref, bf16[8,2,32,512]{3,2,1,0:T(8,128)(2,1)S(1)} %get-tuple-element.135.first_ref, bf16[8,2,32,512]{3,2,1,0:T(8,128)(2,1)S(1)} %get-tuple-element.136.second_ref), custom_call_target="tpu_custom_call" | custom-call | tf_op jit(solution)/shard_map/grams/pallas_call | solution.py:156
  114.4 0.7 copy.70
Async XLA Ops:
  1.3 1.3 %copy-start.1 = (f32[512,4]{0,1:T(4,128)S(1)}, f32[512,4]{0,1:T(4,128)}, u32[]{:S(2)}) copy-start(f32[512,4]{0,1:T(4,128)} %param.66) | copy-start | bytes 24580
  2.8 1.0 copy-start

commit v2 on v0

v2 whole, which is shorter than its diff:
```python
import functools

import jax
import jax.numpy as jnp
from jax import lax
from jax.experimental import pallas as pl
from jax.experimental.pallas import tpu as pltpu
from jax.sharding import PartitionSpec as P

FEATURES = 8192
GROUP = 128
ROUNDS = 2
EPS = 1e-06
N_BLK = 32
NY = 4
MESH = pl.DeviceIdType.MESH
VMEM = pl.BlockSpec(memory_space=pltpu.VMEM)
BF16, F32 = jnp.bfloat16, jnp.float32


def remote(src, dst, send, recv, peer):
    return pltpu.make_async_remote_copy(
        src_ref=src, dst_ref=dst, send_sem=send, recv_sem=recv, device_id=peer, device_id_type=MESH)


def fetch_kernel(offset, low_ref, high_ref, part_ref, other_ref, wide_ref, send, recv, send_y, recv_y):
    blk, feat = lax.axis_index("blk"), lax.axis_index("feat")
    source = lax.rem(blk + offset, N_BLK)
    target = lax.rem(blk + (N_BLK - offset), N_BLK)
    y = lax.rem(feat // 2, NY)
    ys = [lax.rem(y + t, NY) for t in range(NY)]
    feats = [feat + 2 * (there - y) for there in ys]
    barrier = pltpu.get_barrier_semaphore()
    for t in range(NY):
        pl.semaphore_signal(barrier, inc=1, device_id={"blk": source, "feat": feats[t]}, device_id_type=MESH)
    for t in range(1, NY):
        pl.semaphore_signal(barrier, inc=1, device_id={"blk": blk, "feat": feats[t]}, device_id_type=MESH)
    wide_ref[y] = part_ref[...]
    pl.semaphore_wait(barrier, 2 * NY - 1)
    copies = []
    for t in range(NY):
        for h, src in enumerate((low_ref, high_ref)):
            copies.append(remote(src.at[ys[t]], other_ref.at[y, h], send.at[t, h], recv.at[t, h],
                                 {"blk": target, "feat": feats[t]}))
    for t in (1, 3, 2):
        copies.append(remote(part_ref, wide_ref.at[y], send_y.at[t - 1], recv_y.at[t - 1],
                             {"blk": blk, "feat": feats[t]}))
    for copy in copies:
        copy.start()
    for copy in copies:
        copy.wait()


def fetch(offset, low, high, part):
    dma = pltpu.SemaphoreType.DMA
    return pl.pallas_call(
        functools.partial(fetch_kernel, offset),
        out_shape=(jax.ShapeDtypeStruct((NY, 2, 2, 32, 512), BF16), jax.ShapeDtypeStruct((NY, 256, 512), BF16)),
        in_specs=[VMEM] * 3,
        out_specs=(VMEM, VMEM),
        scratch_shapes=[dma((NY, 2)), dma((NY, 2)), dma((NY - 1,)), dma((NY - 1,))],
        compiler_params=pltpu.CompilerParams(collective_id=offset, has_side_effects=True),
        name=f"fetch_{offset}",
    )(low.reshape(NY, 2, 32, 512), high.reshape(NY, 2, 32, 512), part)


def dot_t(a, b):
    return lax.dot_general(a, b, (((1,), (1,)), ((), ())), preferred_element_type=F32)


def square_sums(blocks):
    square = sum(jnp.square(block.astype(F32)) for block in blocks)
    high = square.astype(BF16)
    low = (square - high.astype(F32)).astype(BF16)
    ones = jnp.ones((8, square.shape[1]), BF16)
    return dot_t(ones, high) + dot_t(ones, low)


def gram_kernel(first_ref, second_ref, low_ref, high_ref, out_ref,
                mine, s1, r1, s2, r2, n1, n2, send1, recv1, send2, recv2):
    blk, feat = lax.axis_index("blk"), lax.axis_index("feat")
    core = lax.rem(feat, 2)
    half = feat // 8
    to_core = {"blk": blk, "feat": feat + 1 - 2 * core}
    to_half = {"blk": blk, "feat": feat + 8 - 16 * half}
    barrier = pltpu.get_barrier_semaphore()
    for peer in (to_core, to_half):
        pl.semaphore_signal(barrier, inc=1, device_id=peer, device_id_type=MESH)

    owns = (low_ref, high_ref)
    rows = [jnp.concatenate([ref[y].reshape(128, 512) for ref in (first_ref, second_ref)]) for y in range(NY)]
    stage1, stage2 = [], []
    for a in range(2):
        product = dot_t(rows[0], owns[a][0])
        for y in range(1, NY):
            product = product + dot_t(rows[y], owns[a][y])
        mine[a] = product.reshape(ROUNDS, 2, 2, 32, 256)
        s1[a] = mine[a, :, :, 1 - core].astype(BF16)
        if a == 0:
            pl.semaphore_wait(barrier, 2)
        copy = remote(s1.at[a], r1.at[a], send1.at[a], recv1.at[a], to_core)
        copy.start()
        stage1.append(copy)

    row = lax.broadcasted_iota(jnp.int32, (8, 128), 0)
    sums = [square_sums([owns[a][y] for y in range(NY)]) for a in range(2)]
    lines = [sums[0][:, :128], sums[0][:, 128:], sums[1][:, :128], sums[1][:, 128:]]
    lines += [square_sums([ref[y].reshape(128, 512) for y in range(NY)]) for ref in (first_ref, second_ref)]
    value = lines[0]
    for k in range(1, 6):
        value = jnp.where(row == k, lines[k], value)
    n1[0] = value
    copy = remote(n1.at[0], n1.at[1], send1.at[2], recv1.at[2], to_core)
    copy.start()
    stage1.append(copy)

    for a in range(2):
        stage1[a].wait_recv()
        s2[a] = (mine[a, :, 1 - half, core] + r1[a, :, 1 - half].astype(F32)).astype(BF16)
        copy = remote(s2.at[a], r2.at[a], send2.at[a], recv2.at[a], to_half)
        copy.start()
        stage2.append(copy)
    stage1[2].wait_recv()
    n2[0] = n1[0] + n1[1]
    copy = remote(n2.at[0], n2.at[1], send2.at[2], recv2.at[2], to_half)
    copy.start()
    stage2.append(copy)
    kept = [mine[a, :, half, core] + r1[a, :, half].astype(F32) for a in range(2)]

    stage2[2].wait_recv()
    inverse = lax.rsqrt(n2[0] + n2[1] + EPS)
    lane = lax.broadcasted_iota(jnp.int32, (32, 128), 1)
    at = lax.broadcasted_iota(jnp.int32, (32, 128), 0) + (half * 2 + core) * 32
    factor = F32(FEATURES) ** 0.5
    columns = []
    for r in range(ROUNDS):
        spread = jnp.broadcast_to(inverse[4 + r:5 + r], (32, 128))
        columns.append(jnp.sum(jnp.where(lane == at, spread, 0.0), axis=1, keepdims=True))
    for a in range(2):
        stage2[a].wait_recv()
        gram = kept[a] + r2[a].astype(F32)
        for k in range(2):
            across = inverse[2 * a + k:2 * a + k + 1]
            for r in range(ROUNDS):
                part = gram[r, :, 128 * k:128 * k + 128]
                out_ref[r, :, 256 * a + 128 * k:256 * a + 128 * k + 128] = part * across * columns[r] * factor
    for copy in stage1 + stage2:
        copy.wait_send()


def grams(first, second, low, high):
    dma = pltpu.SemaphoreType.DMA
    return pl.pallas_call(
        gram_kernel,
        out_shape=jax.ShapeDtypeStruct((ROUNDS, 32, 512), F32),
        in_specs=[VMEM] * 4,
        out_specs=VMEM,
        scratch_shapes=[
            pltpu.VMEM((2, ROUNDS, 2, 2, 32, 256), F32),
            pltpu.VMEM((2, ROUNDS, 2, 32, 256), BF16),
            pltpu.VMEM((2, ROUNDS, 2, 32, 256), BF16),
            pltpu.VMEM((2, ROUNDS, 32, 256), BF16),
            pltpu.VMEM((2, ROUNDS, 32, 256), BF16),
            pltpu.VMEM((2, 8, 128), F32),
            pltpu.VMEM((2, 8, 128), F32),
            dma((3,)), dma((3,)), dma((3,)), dma((3,)),
        ],
        compiler_params=pltpu.CompilerParams(
            collective_id=0, has_side_effects=True, vmem_limit_bytes=32 * 1024 * 1024),
        name="grams",
    )(first, second, low, high)


def local(values, scales, pairing):
    rows, width = values.shape
    groups = scales.shape[1]
    wide = values.astype(F32).reshape(rows, groups, width // groups) * scales[:, :, None]
    features = wide.reshape(rows, width).astype(BF16)
    halves = features[:256], features[256:]
    fetches = [functools.partial(fetch, offset) for offset in range(1, N_BLK)]
    (first, low), (second, high) = [
        lax.switch(pairing[r] - 1, fetches, *halves, halves[r]) for r in range(ROUNDS)]
    return jnp.swapaxes(grams(first, second, low, high), 1, 2)


def solution(mesh):
    placed = (P("blk", "feat"), P("blk", "feat"), P())
    return jax.shard_map(
        local, mesh=mesh, in_specs=placed, out_specs=P(None, "blk", "feat"), check_vma=False
    )
```

time: 423 us -> 82.5 us (0.20)
  waiting for transfers between devices: 233 us -> 0 us
  starting transfers between devices: 90.7 us -> 0 us
  Pallas kernels: 0 us -> 77.2 us
  blocking collectives: 71.1 us -> 0 us
  between operations: 20.4 us -> 1.42 us
    ppermute x18 -> x0, waiting for transfers between devices: 118 us -> none  [passed_along(): return lax.ppermute(value, axis, pairs)]
    reduce_scatter x2 -> x0, waiting for transfers between devices: 115 us -> none  [local(): lax.psum_scatter(partial_value.astype(jnp.bfloat16), 'feat', scatter_dime...]
    ppermute x18 -> x0, starting transfers between devices: 90.7 us -> none  [passed_along(): return lax.ppermute(value, axis, pairs)]
    pallas_call x0 -> x3, Pallas kernels: none -> 77.2 us  [the longest x2 56.2 us: fetch(): pl.pallas_call(functools.partial(fetch_kernel, offset), out_shape=(jax.Sh...]
    psum x1 -> x0, blocking collectives: 71.1 us -> none  [local(): other_sq = lax.psum(other_part, 'feat')]
  transfers between devices with their start and end apart: 20 -> 0, of which waited for: 10 -> 0; matrix products, arithmetic and copies ran while one was open for 1% -> 0% of each run, Pallas kernels for 0% -> 0%
where the time goes in v2:
time: 82.5 us; the launch traced here: 82.2 us
  Pallas kernels  77.2 us (94%)
  local copies, waits for them, and re-layouts  3.19 us (4%)
  between operations  1.42 us (2%)
    pallas_call x2, Pallas kernels, fetch(): pl.pallas_call(functools.partial(fetch_kernel, offset), out_shape=(jax.Sh...  56.2 us
    pallas_call x1, Pallas kernels, grams(): pl.pallas_call(gram_kernel, out_shape=jax.ShapeDtypeStruct((ROUNDS, 32, 5...  21 us

profile of v2, /device:TPU:6, one launch (start us, length us, event | category | flops | bytes accessed | tf_op | source)
XLA Modules:
  0.0 82.2 jit_solution(1756883901954711198)
XLA Ops:
  0.0 1.3 %fusion.2 = (s32[1]{0:T(128)}, s32[1]{0:T(128)}) fusion(s32[2]{0:T(128)} %param.67), kind=kLoop, calls=%fused_computation.3 | loop fusion | bytes 16 | tf_op jit(solution)/shard_map/slice | solution.py:182
  1.3 0.0 copy-start.1
  2.7 0.0 copy-done.1
  2.7 0.1 copy.4
  2.8 0.0 copy-start
  2.8 0.6 mul.11
  3.4 0.4 copy-done
  3.9 0.2 fusion
  4.1 28.2 %conditional.3 = ((bf16[4,2,2,32,512]{4,3,2,1,0:T(8,128)(2,1)S(1)}, bf16[4,256,512]{2,1,0:T(8,128)(2,1)S(1)})) conditional(s32[]{:T(128)} %bitcast.125, (bf16[256,512]{1,0:T(8,128)(2,1)S(1)}, bf16[256,512]{1,0:T(8,128)(2,1)S(1)}) %tuple.191, (bf16[256,512]{1,0:T(8,128)(2,1)S(1)}, ...), branch_computations={%region_31.0_spmd, %region_32.0_spmd, %region_33.0_spmd, %region_3... | conditional | bytes 8 | solution.py:182
  4.2 28.1 %fetch_25.3 = (bf16[4,2,2,32,512]{4,3,2,1,0:T(8,128)(2,1)S(1)}, bf16[4,256,512]{2,1,0:T(8,128)(2,1)S(1)}) custom-call(bf16[4,2,32,512]{3,2,1,0:T(8,128)(2,1)S(1)} %bitcast.219, bf16[4,2,32,512]{3,2,1,0:T(8,128)(2,1)S(1)} %bitcast.157, bf16[256,512]{1,0:T(8,128)(2,1)S(1)} %get-tuple-element.364.part_ref), custom_call_target="tpu_custom_call" | custom-call | tf_op jit(solution)/shard_map/cond/branch_24_fun/fetch_25/pallas_call | solution.py:56
  32.3 28.2 %conditional.2 = ((bf16[4,2,2,32,512]{4,3,2,1,0:T(8,128)(2,1)}, bf16[4,256,512]{2,1,0:T(8,128)(2,1)S(1)})) conditional(s32[]{:T(128)} %bitcast.124, (bf16[256,512]{1,0:T(8,128)(2,1)S(1)}, bf16[256,512]{1,0:T(8,128)(2,1)S(1)}) %tuple.191, (bf16[256,512]{1,0:T(8,128)(2,1)S(1)}, ...), branch_computations={%region_0.0_spmd, %region_1.0_spmd, %region_2.0_spmd, %region_3.0_... | conditional | bytes 8 | solution.py:182
  32.4 28.1 %fetch_15.2 = (bf16[4,2,2,32,512]{4,3,2,1,0:T(8,128)(2,1)}, bf16[4,256,512]{2,1,0:T(8,128)(2,1)S(1)}) custom-call(bf16[4,2,32,512]{3,2,1,0:T(8,128)(2,1)S(1)} %bitcast.240, bf16[4,2,32,512]{3,2,1,0:T(8,128)(2,1)S(1)} %bitcast.178, bf16[256,512]{1,0:T(8,128)(2,1)S(1)} %get-tuple-element.281.part_ref), custom_call_target="tpu_custom_call" | custom-call | tf_op jit(solution)/shard_map/cond/branch_14_fun/fetch_15/pallas_call | solution.py:56
  60.5 21.0 %grams.1 = f32[2,32,512]{2,1,0:T(8,128)S(1)} custom-call(bf16[4,2,2,32,512]{4,3,2,1,0:T(8,128)(2,1)} %get-tuple-element.381.first_ref, bf16[4,2,2,32,512]{4,3,2,1,0:T(8,128)(2,1)S(1)} %get-tuple-element.382.second_ref, bf16[4,256,512]{2,1,0:T(8,128)(2,1)S(1)} %get-tuple-element.383.low_ref, bf16[4,256,512]{2,1,0:T(8,128)(2,1)S(1)} %get-tuple-element.384.high_ref), custom_call_target="tpu_custom_call" | custom-call | tf_op jit(solution)/shard_map/grams/pallas_call | solution.py:153
  81.5 0.7 copy.132
  (1 shorter events, 0.0 us)
Async XLA Ops:
  1.3 1.4 %copy-start.1 = (f32[512,4]{0,1:T(4,128)S(1)}, f32[512,4]{0,1:T(4,128)}, u32[]{:S(2)}) copy-start(f32[512,4]{0,1:T(4,128)} %param.66) | copy-start | bytes 24580
  2.8 1.0 %copy-start = (bf16[512,512]{1,0:T(8,128)(2,1)S(1)}, bf16[512,512]{1,0:T(8,128)(2,1)}, u32[]{:S(2)}) copy-start(bf16[512,512]{1,0:T(8,128)(2,1)} %param.65) | copy-start | bytes 1572868

commit v3 on v0

v3 whole, which is shorter than its diff:
```python
import functools

import jax
import jax.numpy as jnp
from jax import lax
from jax.experimental import pallas as pl
from jax.experimental.pallas import tpu as pltpu
from jax.sharding import PartitionSpec as P

FEATURES = 8192
GROUP = 128
ROUNDS = 2
EPS = 1e-06
NX, NZ = 4, 8
NY = 4
MESH = pl.DeviceIdType.MESH
VMEM = pl.BlockSpec(memory_space=pltpu.VMEM)
SMEM = pl.BlockSpec(memory_space=pltpu.SMEM)
BF16, F32 = jnp.bfloat16, jnp.float32


def dot_t(a, b):
    return lax.dot_general(a, b, (((1,), (1,)), ((), ())), preferred_element_type=F32)


def kernel(shifts, pairing_ref, values_ref, scales_ref, out_ref,
           held, piece, near, stage, mine, squares, s1, r1, s2, r2, n1, n2,
           send_p, recv_p, send_x, recv_x, send_w, recv_w, send_z, recv_z, send1, recv1, send2, recv2):
    blk, feat = lax.axis_index("blk"), lax.axis_index("feat")
    x, z = blk // NZ, lax.rem(blk, NZ)
    half, y, core = feat // 8, lax.rem(feat // 2, NY), lax.rem(feat, 2)
    to_core = (blk, feat + 1 - 2 * core)
    to_half = (blk, feat + 8 - 16 * half)
    own = held.at[0, pl.ds(0, 2 * NY)]
    moved = [r for r in range(ROUNDS) if shifts[r]]

    def at_y(t):
        return lax.rem(y + NY - t, NY)

    def to_y(t):
        return (blk, feat + 2 * (at_y(t) - y))

    def to_x(s):
        return (lax.rem(x + NX - s, NX) * NZ + z, feat)

    def to_z(d):
        return (x * NZ + lax.rem(z + NZ - d, NZ), feat)

    barrier = pltpu.get_barrier_semaphore()
    sources = [to_z(NZ - d) for d in sorted(set(shifts)) if d]
    peers = [to_y(t) for t in range(1, NY)] + [to_x(s) for s in range(1, NX)] + sources + [to_core, to_half]
    for peer in peers:
        pl.semaphore_signal(barrier, inc=1, device_id=peer, device_id_type=MESH)

    def remote(src, dst, send, recv, peer):
        return pltpu.make_async_remote_copy(
            src_ref=src, dst_ref=dst, send_sem=send, recv_sem=recv, device_id=peer, device_id_type=MESH)

    def piece_copy(t, h):
        return remote(held.at[0, h * NY + at_y(t)], piece.at[t, h],
                      send_p.at[t - 1, h], recv_p.at[t - 1, h], to_y(t))

    def wide_copy(t):
        return remote(own, held.at[t, pl.ds(0, 2 * NY)], send_w.at[t - 1], recv_w.at[t - 1], to_y(t))

    def x_copy(t, s):
        return remote(piece.at[t], near.at[t, s - 1], send_x.at[t, s - 1], recv_x.at[t, s - 1], to_x(s))

    def z_copy(t, r):
        return remote(stage.at[t, r], held.at[t, pl.ds(2 * NY + 2 * r, 2)], send_z.at[t, r], recv_z.at[t, r],
                      to_z(shifts[r]))

    @pl.loop(0, 2 * NY)
    def _(q):
        rows = pl.ds(q * 64, 64)
        for g in range(values_ref.shape[1] // GROUP):
            lanes = slice(g * GROUP, (g + 1) * GROUP)
            part = (values_ref[rows, lanes].astype(F32) * scales_ref[rows, g:g + 1]).astype(BF16)
            held[0, q, :, :, lanes] = part.reshape(2, 32, GROUP)

    for h in range(2):
        piece[0, h] = held[0, h * NY + y]
    pl.semaphore_wait(barrier, len(peers))

    @pl.loop(1, NY)
    def _(t):
        for h in range(2):
            piece_copy(t, h).start()

    first = pairing_ref[0]
    second = pairing_ref[1]
    swap = lax.rem(first, NZ) > lax.rem(second, NZ)
    offsets = [jnp.where(swap, second, first), jnp.where(swap, first, second)]
    picks = [lax.rem(offsets[r] // NZ + jnp.where(z < shifts[r], 1, 0), NX) for r in range(ROUNDS)]

    @pl.loop(0, NY + 1)
    def _(later):
        @pl.when(jnp.logical_and(later > 0, later < NY))
        def _():
            for h in range(2):
                piece_copy(later, h).wait_recv()

        @pl.when(later < NY)
        def _():
            @pl.loop(1, NX)
            def _(s):
                x_copy(later, s).start()

        @pl.when(later == 0)
        def _():
            @pl.loop(1, NY)
            def _(t):
                wide_copy(t).start()

        @pl.when(later > 0)
        def _():
            t = later - 1

            @pl.loop(1, NX)
            def _(s):
                x_copy(t, s).wait_recv()

            for r in range(ROUNDS):
                @pl.loop(0, 4)
                def _(q):
                    h, c = q // 2, lax.rem(q, 2)
                    value = piece[t, h, c]
                    for s in range(1, NX):
                        value = lax.select(picks[r] == s, near[t, s - 1, h, c], value)
                    if shifts[r]:
                        stage[t, r, h, c] = value
                    else:
                        held[t, 2 * NY + 2 * r + h, c] = value

                if shifts[r]:
                    z_copy(t, r).start()

    @pl.loop(1, NY)
    def _(t):
        wide_copy(t).wait_recv()

    @pl.loop(0, 2)
    def _(k):
        mine[k] = jnp.zeros(mine.shape[1:], F32)

    ones = jnp.ones((8, 512), BF16)
    row = lax.broadcasted_iota(jnp.int32, (8, 128), 0)
    stage1 = remote(s1, r1, send1.at[0], recv1.at[0], to_core)
    n1[0] = jnp.zeros((8, 128), F32)

    @pl.loop(0, 2)
    def _(late):
        @pl.when(late == 1)
        def _():
            @pl.loop(0, NY)
            def _(t):
                for r in moved:
                    z_copy(t, r).wait_recv()
                rows = held[t, pl.ds(2 * NY, 4)].reshape(256, 512)

                @pl.loop(0, 2)
                def _(k):
                    owns = held[t, pl.ds(k * NY, NY)].reshape(256, 512)
                    mine[k] += dot_t(rows, owns).reshape(ROUNDS, 2, 2, 32, 256)

            @pl.loop(0, 2)
            def _(k):
                s1[k] = mine[k, :, :, 1 - core].astype(BF16)

            stage1.start()

        @pl.loop(4 * late, 4 + 2 * late)
        def _(k):
            squares[...] = jnp.zeros_like(squares)

            @pl.loop(0, NY)
            def _(t):
                squares[...] += jnp.square(held[t, pl.ds(2 * k, 2)].reshape(128, 512).astype(F32))

            square = squares[...]
            upper = square.astype(BF16)
            lower = (square - upper.astype(F32)).astype(BF16)
            n1[0] = jnp.where(row == k, dot_t(ones, upper) + dot_t(ones, lower), n1[0])

    norm1 = remote(n1.at[0], n1.at[1], send1.at[1], recv1.at[1], to_core)
    norm1.start()
    stage1.wait_recv()

    @pl.loop(0, 2)
    def _(k):
        s2[k] = (mine[k, :, 1 - half, core] + r1[k, :, 1 - half].astype(F32)).astype(BF16)

    stage2 = remote(s2, r2, send2.at[0], recv2.at[0], to_half)
    stage2.start()
    norm1.wait_recv()
    n2[0] = n1[0] + n1[1]
    norm2 = remote(n2.at[0], n2.at[1], send2.at[1], recv2.at[1], to_half)
    norm2.start()

    norm2.wait_recv()
    inverse = lax.rsqrt(n2[0] + n2[1] + EPS)
    lane = lax.broadcasted_iota(jnp.int32, (32, 128), 1)
    at = lax.broadcasted_iota(jnp.int32, (32, 128), 0) + (half * 2 + core) * 32
    factor = F32(FEATURES) ** 0.5
    columns = []
    for r in range(ROUNDS):
        spread = jnp.broadcast_to(inverse[4 + r:5 + r], (32, 128))
        columns.append(jnp.sum(jnp.where(lane == at, spread, 0.0), axis=1, keepdims=True))
    stage2.wait_recv()
    for k in range(4):
        lanes = slice(128 * (k % 2), 128 * (k % 2) + 128)
        tiles = []
        for r in range(ROUNDS):
            gram = mine[k // 2, r, half, core, :, lanes] + r1[k // 2, r, half, :, lanes].astype(F32)
            gram = gram + r2[k // 2, r, :, lanes].astype(F32)
            tiles.append(gram * inverse[k:k + 1] * columns[r] * factor)
        lanes = slice(128 * k, 128 * k + 128)
        out_ref[0, :, lanes] = lax.select(swap, tiles[1], tiles[0])
        out_ref[1, :, lanes] = lax.select(swap, tiles[0], tiles[1])

    for copy in (stage1, norm1, stage2, norm2):
        copy.wait_send()

    @pl.loop(0, NY)
    def _(t):
        @pl.when(t > 0)
        def _():
            wide_copy(t).wait_send()
            for h in range(2):
                piece_copy(t, h).wait_send()

        @pl.loop(1, NX)
        def _(s):
            x_copy(t, s).wait_send()

        for r in moved:
            z_copy(t, r).wait_send()


def tiles(number, shifts, pairing, values, scales):
    dma = pltpu.SemaphoreType.DMA
    rows = (2, 2, 32, 512)
    return pl.pallas_call(
        functools.partial(kernel, shifts),
        out_shape=jax.ShapeDtypeStruct((ROUNDS, 32, 512), F32),
        in_specs=[SMEM, VMEM, VMEM],
        out_specs=VMEM,
        scratch_shapes=[
            pltpu.VMEM((NY, 2 * NY + 2 * ROUNDS, 2, 32, 512), BF16),
            pltpu.VMEM((NY,) + rows, BF16),
            pltpu.VMEM((NY, NX - 1) + rows, BF16),
            pltpu.VMEM((NY, ROUNDS) + rows, BF16),
            pltpu.VMEM((2, ROUNDS, 2, 2, 32, 256), F32),
            pltpu.VMEM((128, 512), F32),
            pltpu.VMEM((2, ROUNDS, 2, 32, 256), BF16),
            pltpu.VMEM((2, ROUNDS, 2, 32, 256), BF16),
            pltpu.VMEM((2, ROUNDS, 32, 256), BF16),
            pltpu.VMEM((2, ROUNDS, 32, 256), BF16),
            pltpu.VMEM((2, 8, 128), F32),
            pltpu.VMEM((2, 8, 128), F32),
            dma((NY - 1, 2)), dma((NY - 1, 2)),
            dma((NY, NX - 1)), dma((NY, NX - 1)),
            dma((NY - 1,)), dma((NY - 1,)),
            dma((NY, ROUNDS)), dma((NY, ROUNDS)),
            dma((2,)), dma((2,)), dma((2,)), dma((2,)),
        ],
        compiler_params=pltpu.CompilerParams(
            collective_id=number, has_side_effects=True, vmem_limit_bytes=32 * 1024 * 1024),
        name=f"tiles_{shifts[0]}_{shifts[1]}",
    )(pairing, values, scales)


def local(values, scales, pairing):
    cases = [(low, high) for high in range(NZ) for low in range(high + 1)]
    digits = jnp.bitwise_and(pairing, NZ - 1)
    swapped = digits[::-1]
    low, high = jnp.minimum(digits, swapped), jnp.maximum(digits, swapped)
    case = (jnp.right_shift(high * (high + 1), 1) + low)[0]
    branches = [functools.partial(tiles, number, shifts) for number, shifts in enumerate(cases)]
    return jnp.swapaxes(lax.switch(case, branches, pairing, values, scales), 1, 2)


def solution(mesh):
    placed = (P("blk", "feat"), P("blk", "feat"), P())
    return jax.shard_map(
        local, mesh=mesh, in_specs=placed, out_specs=P(None, "blk", "feat"), check_vma=False
    )
```

time: 423 us -> 72.5 us (0.17)
  the two profiles are of different devices: /device:TPU:6 before, /device:TPU:1 now
where the time goes in v3:
time: 72.5 us; the launch traced here: 72.3 us
  Pallas kernels  70 us (97%)
  local copies, waits for them, and re-layouts  1.56 us (2%)
    pallas_call x1, Pallas kernels, tiles(): pl.pallas_call(functools.partial(kernel, shifts), out_shape=jax.ShapeDtyp...  70 us

profile of v3, /device:TPU:1, one launch (start us, length us, event | category | flops | bytes accessed | tf_op | source)
XLA Modules:
  0.0 72.3 jit_solution(10037828306994818263)
XLA Ops:
  0.0 0.0 copy-start.1
  0.0 0.0 copy-start
  0.0 0.7 copy-done.1
  0.7 0.1 reverse.3
  0.8 0.0 copy-done
  0.8 70.8 %conditional.1 = (f32[2,32,512]{2,1,0:T(8,128)S(1)}) conditional(s32[]{:T(128)} %bitcast, (s32[2]{0:T(128)S(1)}, bf16[512,512]{1,0:T(8,128)(2,1)}, f32[512,4]{0,1:T(4,128)S(1)}) %tuple.239, (s32[2]{0:T(128)S(1)}, bf16[512,512]{1,0:T(8,128)(2,1)}, f32[512,4]{0,1:T(4,128)S(1)}) %tuple.257, (s32[2]{0:T(128)S(1)}, ...), branch_computations={%region_0.0_spmd, %region_1.0_spmd, %region_2.0_spmd, %region_3.0_... | conditional | bytes 16392 | solution.py:280
  0.9 0.1 copy.8.scales_ref
  1.0 70.0 %tiles_1_2.1 = f32[2,32,512]{2,1,0:T(8,128)S(1)} custom-call(s32[2]{0:T(128)S(1)} %get-tuple-element.248.pairing_ref, bf16[512,512]{1,0:T(8,128)(2,1)} %get-tuple-element.249.values_ref, f32[512,4]{1,0:T(8,128)S(1)} %copy.8.scales_ref), custom_call_target="tpu_custom_call" | custom-call | tf_op jit(solution)/shard_map/cond/branch_4_fun/tiles_1_2/pallas_call | solution.py:243
  71.6 0.7 copy.77
  (1 shorter events, 0.0 us)
Async XLA Ops:
  0.0 0.7 copy-start.1
  0.0 0.8 %copy-start = (f32[512,4]{0,1:T(4,128)S(1)}, f32[512,4]{0,1:T(4,128)}, u32[]{:S(2)}) copy-start(f32[512,4]{0,1:T(4,128)} %param.40) | copy-start | bytes 24580
